TPU v7x, 256 devices: a whole 4x4x8 slice. The times are simulated.
256 devices in a mesh: rep: 2 (over y_lo), wide: 16 (over z, core), narrow: 8 (over y_hi, x).
Axes of the slice: x: 4, y: 4 (y_hi: 2, y_lo: 2; y = y_hi * 2 + y_lo), z: 8, core: 2. Of those that a mesh axis runs over, the one named last changes fastest.
Arguments:
- tokens: bfloat16 [256, 256, 1280], P(('rep', 'wide', 'narrow')), may hold values from -24 to 24
- routing: bfloat16 [1280, 128], replicated, may hold values from -1 to 1
- grad_out: bfloat16 [256, 256, 1280], P(('rep', 'wide', 'narrow')), may hold values from -1.5 to 1.5
- slot_out: bfloat16 [256, 128, 1280], P(('rep', 'wide', 'narrow')), may hold values from -6 to 6
- w_first: bfloat16 [64, 1280, 4096], P(('rep', 'wide'), None, 'narrow'), may hold values from -0.15625 to 0.15625
- w_second: bfloat16 [64, 4096, 1280], P(('rep', 'wide'), 'narrow'), may hold values from -0.09375 to 0.09375
Outputs:
- grad_tokens: bfloat16 [256, 256, 1280], P(('rep', 'wide', 'narrow'))
- grad_routing: float32 [1280, 128], P(('rep', 'wide', 'narrow'))
- grad_first: bfloat16 [64, 1280, 4096], P(('rep', 'wide'), None, 'narrow')
- grad_second: bfloat16 [64, 4096, 1280], P(('rep', 'wide'), 'narrow')
All inputs are finite; a program needn't handle non-finite values.
Results may differ from a plain program's by a relative error of at most 0.023.
Values may be sent and summed in bfloat16 or wider, within the bound.
A program may use at most 64 MiB of HBM per device.

v0:
```python
import jax
import jax.numpy as jnp
from jax import lax
from jax.sharding import PartitionSpec as P

root_half = 0.7071067811865476
density_scale = 0.3989422804014327


def soft_max(values, over_dim):
    largest = jnp.max(values, axis=over_dim, keepdims=True)
    powers = jnp.exp(values - largest)
    return powers / jnp.sum(powers, axis=over_dim, keepdims=True)


def gelu_pair(hidden):
    normal_cdf = 0.5 * (1.0 + jax.scipy.special.erf(hidden * root_half))
    density = density_scale * jnp.exp(-0.5 * hidden * hidden)
    return (hidden * normal_cdf, normal_cdf + hidden * density)


def contract_first(left_op, right_op):
    return lax.dot_general(
        left_op, right_op, (((0,), (0,)), ((), ())), preferred_element_type=jnp.float32
    )


def contract_last(left_op, right_op):
    return lax.dot_general(
        left_op, right_op, (((1,), (1,)), ((), ())), preferred_element_type=jnp.float32
    )


def local(tokens, routing, grad_out, slot_out, w_first, w_second):
    image_x = tokens[0]
    image_dy = grad_out[0]
    image_out = slot_out[0]
    width = image_x.shape[1]
    logits = jnp.dot(image_x, routing, preferred_element_type=jnp.float32)
    dispatch = soft_max(logits, 0)
    combine = soft_max(logits, 1)
    dispatch_bf = dispatch.astype(jnp.bfloat16)
    combine_bf = combine.astype(jnp.bfloat16)
    slot_in = contract_first(dispatch_bf, image_x).astype(jnp.bfloat16)
    slot_grad = contract_first(combine_bf, image_dy).astype(jnp.bfloat16)
    groups = lax.axis_size(("rep", "wide"))
    narrow = lax.axis_size("narrow")
    experts_here = w_first.shape[0]
    per_group = slot_in.shape[0] // groups
    slot_count = per_group // experts_here
    routed = (
        lax.all_to_all(slot_in, ("rep", "wide"), split_axis=0, concat_axis=0, tiled=True),
        lax.all_to_all(slot_grad, ("rep", "wide"), split_axis=0, concat_axis=0, tiled=True),
    )
    rows_in, rows_grad = (
        lax.all_gather(routed[0], "narrow", axis=0, tiled=True),
        lax.all_gather(routed[1], "narrow", axis=0, tiled=True),
    )
    rows_in = rows_in.reshape(narrow * groups, experts_here, slot_count, width)
    rows_grad = rows_grad.reshape(narrow * groups, experts_here, slot_count, width)
    pre_act = jnp.einsum("ijsd,jdf->ijsf", rows_in, w_first, preferred_element_type=jnp.float32)
    act_val, act_slope = gelu_pair(pre_act)
    act_bf = act_val.astype(jnp.bfloat16)
    act_grad = jnp.einsum("ijsd,jfd->ijsf", rows_grad, w_second, preferred_element_type=jnp.float32)
    hid_grad = (act_grad * act_slope).astype(jnp.bfloat16)
    grad_second = jnp.einsum(
        "ijsf,ijsd->jfd", act_bf, rows_grad, preferred_element_type=jnp.float32
    ).astype(jnp.bfloat16)
    grad_first = jnp.einsum(
        "ijsd,ijsf->jdf", rows_in, hid_grad, preferred_element_type=jnp.float32
    ).astype(jnp.bfloat16)
    summed = lax.psum_scatter(
        jnp.einsum("ijsf,jdf->ijsd", hid_grad, w_first, preferred_element_type=jnp.float32).astype(
            jnp.bfloat16
        ),
        "narrow",
        scatter_dimension=0,
        tiled=True,
    )
    back_in = summed.reshape(groups * per_group, width)
    slot_back = lax.all_to_all(back_in, ("rep", "wide"), split_axis=0, concat_axis=0, tiled=True)
    comb_raw = contract_last(image_dy, image_out)
    logit_comb = combine * (comb_raw - jnp.sum(combine * comb_raw, axis=1, keepdims=True))
    disp_raw = contract_last(image_x, slot_back)
    logit_disp = dispatch * (disp_raw - jnp.sum(dispatch * disp_raw, axis=0, keepdims=True))
    logit_grad = (logit_comb + logit_disp).astype(jnp.bfloat16)
    grad_x = (
        contract_last(logit_grad, routing)
        + jnp.dot(dispatch_bf, slot_back, preferred_element_type=jnp.float32)
    ).astype(jnp.bfloat16)
    routing_term = contract_first(image_x, logit_grad)
    grad_routing = lax.psum_scatter(
        routing_term, ("rep", "wide", "narrow"), scatter_dimension=0, tiled=True
    )
    return (grad_x[None], grad_routing, grad_first, grad_second)


def solution(mesh):
    return jax.shard_map(
        local,
        mesh=mesh,
        in_specs=(
            P(("rep", "wide", "narrow"), None, None),
            P(),
            P(("rep", "wide", "narrow"), None, None),
            P(("rep", "wide", "narrow"), None, None),
            P(("rep", "wide"), None, "narrow"),
            P(("rep", "wide"), "narrow", None),
        ),
        out_specs=(
            P(("rep", "wide", "narrow"), None, None),
            P(("rep", "wide", "narrow"), None),
            P(("rep", "wide"), None, "narrow"),
            P(("rep", "wide"), "narrow", None),
        ),
        check_vma=False,
    )
```

profile of v0, /device:TPU:1, one launch (start us, length us, event | category | flops | bytes accessed | tf_op | source)
XLA Modules:
  0.0 546.6 jit_solution(11342154472189496175)
XLA Ops:
  7.2 1.7 fusion.45
  9.1 1.4 convolution_convert_fusion.1
  10.6 23.9 %all_to_all.36 = bf16[32,4,1280]{2,1,0:T(4,128)(2,1)S(1)} all-to-all(bf16[32,4,1280]{2,1,0:T(4,128)(2,1)S(1)} %all_to_all.27), channel_id=1, replica_groups=mesh['rep'=2,'wide'=16,'narrow'=8] {'rep','wide'}, dimensions={0} | all-to-all | bytes 655360 | tf_op jit(solution)/shard_map/all_to_all | solution.py:52
  34.5 0.8 all_to_all.29
  35.4 1.5 convolution_convert_fusion.2
  37.0 17.6 %all_to_all.37 = bf16[32,4,1280]{2,1,0:T(4,128)(2,1)S(1)} all-to-all(bf16[32,4,1280]{2,1,0:T(4,128)(2,1)S(1)} %all_to_all.24), channel_id=1, replica_groups=mesh['rep'=2,'wide'=16,'narrow'=8] {'rep','wide'}, dimensions={0} | all-to-all | bytes 655360 | tf_op jit(solution)/shard_map/all_to_all | solution.py:53
  54.5 0.8 all_to_all.26
  55.4 41.6 %all-gather.5.cloned.1.call-done = bf16[1024,1280]{1,0:T(8,128)(2,1)} async-done(((bf16[128,1280]{1,0:T(8,128)(2,1)}), bf16[1024,1280]{1,0:T(8,128)(2,1)}) %all-gather.5.cloned.1.call-update) | async-done | bytes 2621456 | tf_op jit(solution)/shard_map/all_gather | solution.py:56
  97.0 6.4 %reshape.29 = bf16[256,2,2,1280]{3,2,1,0:T(2,128)(2,1)} reshape(bf16[1024,1280]{1,0:T(8,128)(2,1)} %all-gather.5.cloned.1.call-done) | data formatting | bytes 5242880 | tf_op jit(solution)/shard_map/reshape | solution.py:59
  103.4 7.4 %copy.32 = bf16[256,2,2,1280]{0,3,2,1:T(8,128)(2,1)} copy(bf16[256,2,2,1280]{3,2,1,0:T(2,128)(2,1)} %reshape.29) | data formatting | bytes 5242880 | tf_op jit(solution)/shard_map/reshape | solution.py:59
  110.8 4.8 fusion.2
  115.6 47.4 %all-gather.3.cloned.1.call-done = bf16[1024,1280]{1,0:T(8,128)(2,1)} async-done(((bf16[128,1280]{1,0:T(8,128)(2,1)}), bf16[1024,1280]{1,0:T(8,128)(2,1)}) %all-gather.3.cloned.1.call-update) | async-done | bytes 2621456 | tf_op jit(solution)/shard_map/all_gather | solution.py:57
  163.0 6.4 %reshape.28 = bf16[256,2,2,1280]{3,2,1,0:T(2,128)(2,1)} reshape(bf16[1024,1280]{1,0:T(8,128)(2,1)} %all-gather.3.cloned.1.call-done) | data formatting | bytes 5242880 | tf_op jit(solution)/shard_map/reshape | solution.py:60
  169.4 5.2 fusion.15
  174.6 1.0 copy-done.7
  175.6 3.1 fusion
  178.7 81.2 %reduce-scatter.3.cloned.1.call-done = bf16[32,2,2,1280]{3,0,2,1:T(8,128)(2,1)} async-done(((bf16[256,2,2,1280]{3,0,2,1:T(8,128)(2,1)}), bf16[32,2,2,1280]{3,0,2,1:T(8,128)(2,1)}) %reduce-scatter.3.cloned.1.call-update) | async-done | bytes 327696 | tf_op jit(solution)/shard_map/reduce_scatter | solution.py:72
  259.9 2.0 copy.30
  261.8 9.3 %all-to-all-start.2 = ((bf16[32,4,1280]{2,1,0:T(4,128)(2,1)}), bf16[32,4,1280]{2,1,0:T(4,128)(2,1)}, u32[]{:S(2)}, u32[]{:S(2)}) async-start(bf16[32,4,1280]{2,1,0:T(4,128)(2,1)} %copy.30), calls=%async_computation.3 | async-start | bytes 655360 | tf_op jit(solution)/shard_map/all_to_all | solution.py:81
  271.4 5.2 bitcast_convert_fusion.1
  276.6 2.9 bitcast_convert_fusion
  279.6 4.6 all-to-all-done.2
  284.2 1.8 all_to_all.32
  286.0 1.3 convolution_bitcast_fusion.1
  287.3 1.6 multiply_reduce_fusion.1
  288.9 0.6 copy-done.3
  289.5 1.3 convolution_bitcast_fusion
  290.9 1.5 fusion.46
  292.4 2.1 fusion.7
  294.5 243.9 %all-reduce.3.cloned.1.call-done = f32[1280,128]{0,1:T(8,128)} async-done(((f32[1280,128]{0,1:T(8,128)}), f32[1280,128]{0,1:T(8,128)}) %all-reduce.3.cloned.1.call-update) | async-done | bytes 655376
  538.4 1.0 constant_dynamic-slice_fusion
  539.4 0.7 copy.35
  (25 shorter events, 0.8 us)
Async XLA Ops:
  7.2 103.6 %copy-start = (bf16[2,1280,512]{2,1,0:T(8,128)(2,1)S(1)}, bf16[2,1280,512]{2,1,0:T(8,128)(2,1)}, u32[]{:S(2)}) copy-start(bf16[2,1280,512]{2,1,0:T(8,128)(2,1)} %param.10) | copy-start | bytes 7864324
  7.2 89.8 %all-gather.5.cloned.1.call-start = ((), (), s32[]{:S(2)}) async-start(), calls=%async_computation.5 | async-start | bytes 2949120 | tf_op jit(solution)/shard_map/all_gather | solution.py:56
  35.3 127.6 %all-gather.3.cloned.1.call-start = ((), (), s32[]{:S(2)}) async-start(), calls=%async_computation.4 | async-start | bytes 2949120 | tf_op jit(solution)/shard_map/all_gather | solution.py:57
  55.4 204.5 %reduce-scatter.3.cloned.1.call-start = ((), (), s32[]{:S(2)}) async-start(), calls=%async_computation.6 | async-start | bytes 2949120 | tf_op jit(solution)/shard_map/reduce_scatter | solution.py:72
  174.6 1.0 copy-start.7
  261.8 22.4 %all-to-all-start.2 = ((bf16[32,4,1280]{2,1,0:T(4,128)(2,1)}), bf16[32,4,1280]{2,1,0:T(4,128)(2,1)}, u32[]{:S(2)}, u32[]{:S(2)}) async-start(bf16[32,4,1280]{2,1,0:T(4,128)(2,1)} %copy.30), calls=%async_computation.3 | async-start | bytes 655360 | tf_op jit(solution)/shard_map/all_to_all | solution.py:81
  271.2 267.2 %all-reduce.3.cloned.1.call-start = ((), (), s32[]{:S(2)}) async-start(), calls=%async_computation.7 | async-start | bytes 1310720
  271.4 5.2 copy-start.2
  271.4 5.2 copy-start.6
  276.6 9.4 %copy-start.1 = (bf16[1,256,1280]{2,1,0:T(8,128)(2,1)S(1)}, bf16[1,256,1280]{2,1,0:T(8,128)(2,1)}, u32[]{:S(2)}) copy-start(bf16[1,256,1280]{2,1,0:T(8,128)(2,1)} %param.6) | copy-start | bytes 1966084
  288.9 0.7 copy-start.3
  288.9 0.7 copy-start.4
  288.9 0.6 copy-start.5
Sparse Core Ops, SparseCore 0:
  35.5 61.4 all-gather.4
  100.1 62.7 all-gather.2
  178.8 80.9 reduce-scatter.2
  291.0 247.3 all-reduce.2
where the time goes:
time: 548 us; the launch traced here: 547 us
  waiting for transfers between devices  419 us (76%)
  blocking collectives  41.5 us (8%)
  matrix products  33.6 us (6%)
  local copies, waits for them, and re-layouts  29.1 us (5%)
  between operations  13.9 us (3%)
  starting transfers between devices  9.69 us (2%)
    unnamed x5, waiting for transfers between devices  244 us
    reduce_scatter x1, waiting for transfers between devices, local(): lax.psum_scatter(jnp.einsum('ijsf,jdf->ijsd', hid_grad, w_first, preferre...  81.2 us
    all_gather x1, waiting for transfers between devices, local(): lax.all_gather(routed[1], 'narrow', axis=0, tiled=True)  47.4 us
    all_gather x1, waiting for transfers between devices, local(): lax.all_gather(routed[0], 'narrow', axis=0, tiled=True)  41.6 us
    all_to_all x1, blocking collectives, local(): lax.all_to_all(slot_in, ('rep', 'wide'), split_axis=0, concat_axis=0, til...  23.9 us
    all_to_all x1, blocking collectives, local(): lax.all_to_all(slot_grad, ('rep', 'wide'), split_axis=0, concat_axis=0, t...  17.6 us
    reshape x2, local copies, waits for them, and re-layouts, local(): rows_in = rows_in.reshape(narrow * groups, experts_here, slot_count, width)  13.8 us
  transfers between devices with their start and end apart: 5, of which 5 were waited for; matrix products, arithmetic and copies ran while one was open for 6% of the time, Pallas kernels for 0%

commit v1 on v0

v1 whole, which is shorter than its diff:
```python
import functools

import jax
import jax.numpy as jnp
from jax import lax
from jax.experimental import pallas as pl
from jax.experimental.pallas import tpu as pltpu
from jax.sharding import PartitionSpec as P

MESH = pl.DeviceIdType.MESH
BF = jnp.bfloat16
F32 = jnp.float32
root_half = 0.7071067811865476
density_scale = 0.3989422804014327
D = 1280
HALF = 640


def nn(a, b):
    return lax.dot_general(a, b, (((1,), (0,)), ((), ())), preferred_element_type=F32)


def nt(a, b):
    return lax.dot_general(a, b, (((1,), (1,)), ((), ())), preferred_element_type=F32)


def tn(a, b):
    return lax.dot_general(a, b, (((0,), (0,)), ((), ())), preferred_element_type=F32)


def one_hot(rows, cols, pick):
    row = lax.broadcasted_iota(jnp.int32, (rows, cols), 0)
    col = lax.broadcasted_iota(jnp.int32, (rows, cols), 1)
    return (col == pick(row)).astype(F32).astype(BF)


def kernel(
    tok_h, routing_h, gout_h, sout_h, w1_h, w2_h,
    gx_h, gr_ref, g1_h, g2_h,
    tok, routing, gout, sout, w1, w2, gx, g1, g2,
    dispatch, combine, lcomb,
    zs, zr, ai, xg, rows, act, hid, pb, xr1, xr2, xs, yr, bb, zbs, zbr,
    rt, rr1, hh, rr2, gg, rr3, ex, rr4,
    ld_sem, out_sem, loc_sem,
    zf_s, zf_r, yi_s, yi_r, xi_s, xi_r, xg_s, xg_r, yg_s, yg_r,
    rx_s, rx_r, ry_s, ry_r, zb_s, zb_r,
    c_s, c_r, s2_s, s2_r, s3_s, s3_r, s4_s, s4_r,
):
    rep = lax.axis_index("rep")
    wide = lax.axis_index("wide")
    nar = lax.axis_index("narrow")
    x = nar % 4
    y = (nar // 4) * 2 + rep
    z = wide // 2
    c = wide % 2

    def dev_x(d):
        return (rep, wide, (nar // 4) * 4 + (x + d) % 4)

    def dev_y(d):
        yy = (y + d) % 4
        return (yy % 2, wide, (yy // 2) * 4 + x)

    def dev_w(k):
        return (rep, (wide + k) % 16, nar)

    core_dev = (rep, z * 2 + 1 - c, nar)

    def rc(src, dst, ss, rs, dev):
        return pltpu.make_async_remote_copy(
            src_ref=src, dst_ref=dst, send_sem=ss, recv_sem=rs, device_id=dev, device_id_type=MESH
        )

    pending = []

    def go(copy):
        copy.start()
        pending.append(copy)
        return copy

    loads = [
        pltpu.make_async_copy(h, v, ld_sem.at[i])
        for i, (h, v) in enumerate(
            ((tok_h.at[0], tok), (routing_h, routing), (gout_h.at[0], gout), (sout_h.at[0], sout), (w1_h, w1), (w2_h, w2))
        )
    ]
    for copy in loads:
        copy.start()

    barrier = pltpu.get_barrier_semaphore()

    def greet(dev):
        pl.semaphore_signal(barrier, inc=1, device_id=dev, device_id_type=MESH)

    @pl.loop(1, 16)
    def _(k):
        greet(dev_w(k))

    for d in (1, 2, 3):
        greet(dev_x(d))
        greet(dev_y(d))

    @pl.loop(0, 8)
    def _(k):
        @pl.when(jnp.logical_or(nar != z, k != z))
        def _():
            greet((rep, k * 2 + c, z))

    loads[0].wait()
    loads[1].wait()
    logits = nn(tok[...], routing[...])
    e0 = jnp.exp(logits - jnp.max(logits, axis=0, keepdims=True))
    dis = e0 / jnp.sum(e0, axis=0, keepdims=True)
    dispatch[...] = dis
    e1 = jnp.exp(logits - jnp.max(logits, axis=1, keepdims=True))
    com = e1 / jnp.sum(e1, axis=1, keepdims=True)
    combine[...] = com
    dis_bf = dis.astype(BF)
    com_bf = com.astype(BF)
    loads[2].wait()

    def z_copy(j, k):
        to = (wide + k) % 16
        return rc(zs.at[j, to], zr.at[j, wide], zf_s.at[j, k], zf_r.at[j, k], dev_w(k))

    for j in range(2):
        pt = one_hot(
            128, 128,
            lambda s: ((s >> 1) & 1) * 64 + (s >> 3) * 4 + j * 2 + (s & 1),
        )
        first = (lax.broadcasted_iota(jnp.int32, (128, HALF), 0) & 4) == 0
        parts = []
        for probs, src in ((dis_bf, tok), (com_bf, gout)):
            pick = nt(pt, probs).astype(BF)
            both = jnp.where(first, nn(pick, src[:, :HALF]), nn(pick, src[:, HALF:]))
            parts.append(both.reshape(16, 8, HALF))
        zs[j] = jnp.concatenate(parts, axis=1).astype(BF)
        if j == 0:
            pl.semaphore_wait(barrier, 15 + 6 + 7 + (nar != z).astype(jnp.int32))

        @pl.loop(1, 16)
        def _(k):
            z_copy(j, k).start()

        zr[j, wide] = zs[j, wide]

    def z_done(j):
        @pl.loop(1, 16)
        def _(k):
            z_copy(j, k).wait_recv()

    def spread(j):
        m = one_hot(
            256, 256,
            lambda r: ((r >> 1) & 15) * 16 + (r >> 7) * 8 + ((r >> 6) & 1) * 4 + ((r >> 5) & 1) * 2 + (r & 1),
        )
        out = nn(m, zr[j].reshape(256, HALF)).astype(BF)
        for h in range(2):
            cols = slice(h * HALF, (h + 1) * HALF)
            ai[j, :, :, cols] = out[h * 64:h * 64 + 64].reshape(2, 32, HALF)
            xg[j, x, :, :, cols] = out[128 + h * 64:128 + h * 64 + 64].reshape(2, 32, HALF)
        rows[j, 0, x, y] = ai[j, rep]

    def yin_send(j):
        return [
            go(rc(ai.at[j, (y + d) % 2], rows.at[j, 0, x, y], yi_s.at[j, d], yi_r.at[j, d], dev_y(d)))
            for d in (1, 3, 2)
        ]

    def xg_send(j):
        return [
            go(rc(xg.at[j, x], xg.at[j, x], xg_s.at[j, d], xg_r.at[j, d], dev_x(d)))
            for d in (1, 3)
        ]

    def xg_fwd(j):
        a, b = (x + 3) % 4, (x + 1) % 4
        return [
            go(rc(xg.at[j, a, 0], xg.at[j, a, 0], xg_s.at[j, 0], xg_r.at[j, 0], dev_x(1))),
            go(rc(xg.at[j, b, 1], xg.at[j, b, 1], xg_s.at[j, 2], xg_r.at[j, 2], dev_x(3))),
        ]

    def yg_send(j):
        out = [
            go(rc(xg.at[j, :, (y + d) % 2], rows.at[j, 1, :, y], yg_s.at[j, d], yg_r.at[j, d], dev_y(d)))
            for d in (1, 3, 2)
        ]
        own = pltpu.make_async_copy(xg.at[j, :, rep], rows.at[j, 1, :, y], loc_sem.at[j])
        own.start()
        return out, own

    def xin_send(j):
        return [
            go(rc(rows.at[j, 0, x], rows.at[j, 0, x], xi_s.at[j, d], xi_r.at[j, d], dev_x(d)))
            for d in (1, 3)
        ]

    def xin_fwd(j):
        a, b = (x + 3) % 4, (x + 1) % 4
        lo, hi = pl.ds(0, 2), pl.ds(2, 2)
        return [
            go(rc(rows.at[j, 0, a, lo], rows.at[j, 0, a, lo], xi_s.at[j, 0], xi_r.at[j, 0], dev_x(1))),
            go(rc(rows.at[j, 0, b, hi], rows.at[j, 0, b, hi], xi_s.at[j, 2], xi_r.at[j, 2], dev_x(3))),
        ]

    def arrive(copies):
        for copy in copies:
            copy.wait_recv()

    def hidden(j):
        @pl.loop(0, 2)
        def _(i):
            cols = pl.ds(pl.multiple_of(i * 256, 256), 256)
            pre = nn(rows[j, 0].reshape(512, D), w1[j, :, cols])
            cdf = 0.5 * (1.0 + lax.erf(pre * root_half))
            act[j, :, cols] = (pre * cdf).astype(BF)
            slope = cdf + pre * (density_scale * jnp.exp(-0.5 * pre * pre))
            grad = nt(rows[j, 1].reshape(512, D), w2[j, cols, :])
            hid[j, :, cols] = (grad * slope).astype(BF)

    def partial(j):
        @pl.loop(0, 5)
        def _(i):
            cols = pl.ds(pl.multiple_of(i * 256, 256), 256)
            pb[j, :, :, :, cols] = nt(hid[j], w1[j, cols, :]).astype(BF).reshape(4, 4, 32, 256)

    def grads(j):
        @pl.loop(0, 5)
        def _(i):
            cols = pl.ds(pl.multiple_of(i * 256, 256), 256)
            g1[j, cols, :] = tn(rows[j, 0, :, :, :, cols].reshape(512, 256), hid[j]).astype(BF)
            g2[j, :, cols] = tn(act[j], rows[j, 1, :, :, :, cols].reshape(512, 256)).astype(BF)
        a = pltpu.make_async_copy(g1.at[j], g1_h.at[j], out_sem.at[2 * j])
        b = pltpu.make_async_copy(g2.at[j], g2_h.at[j], out_sem.at[2 * j + 1])
        a.start()
        b.start()
        return [a, b]

    lo, hi = pl.ds(0, 2), pl.ds(2, 2)

    def xr_send(j):
        far, up, dn = (x + 2) % 4, (x + 1) % 4, (x + 3) % 4
        first = [
            go(rc(pb.at[j, far, lo], xr1.at[j, 0], rx_s.at[j, 0], rx_r.at[j, 0], dev_x(1))),
            go(rc(pb.at[j, far, hi], xr1.at[j, 1], rx_s.at[j, 1], rx_r.at[j, 1], dev_x(3))),
        ]
        second = [
            go(rc(pb.at[j, up, hi], xr2.at[j, 0, hi], rx_s.at[j, 2], rx_r.at[j, 2], dev_x(1))),
            go(rc(pb.at[j, dn, lo], xr2.at[j, 1, lo], rx_s.at[j, 3], rx_r.at[j, 3], dev_x(3))),
        ]
        return first, second

    def xr_fwd(j):
        up, dn = (x + 1) % 4, (x + 3) % 4
        pb[j, up, lo] = (pb[j, up, lo].astype(F32) + xr1[j, 0].astype(F32)).astype(BF)
        a = go(rc(pb.at[j, up, lo], xr2.at[j, 0, lo], rx_s.at[j, 4], rx_r.at[j, 4], dev_x(1)))
        pb[j, dn, hi] = (pb[j, dn, hi].astype(F32) + xr1[j, 1].astype(F32)).astype(BF)
        b = go(rc(pb.at[j, dn, hi], xr2.at[j, 1, hi], rx_s.at[j, 5], rx_r.at[j, 5], dev_x(3)))
        return [a, b]

    def yr_send(j):
        xs[j] = (pb[j, x].astype(F32) + xr2[j, 0].astype(F32) + xr2[j, 1].astype(F32)).astype(BF)
        return [
            go(rc(xs.at[j, (y + d) % 4], yr.at[j, d - 1], ry_s.at[j, d], ry_r.at[j, d], dev_y(d)))
            for d in (1, 3, 2)
        ]

    def yr_sum(j):
        bb[0, j] = (xs[j, y].astype(F32) + yr[j, 1].astype(F32)).astype(BF)
        bb[1, j] = (yr[j, 0].astype(F32) + yr[j, 2].astype(F32)).astype(BF)

    loads[3].wait()
    comb_raw = nt(gout[...], sout[...])
    com = combine[...]
    lcomb[...] = com * (comb_raw - jnp.sum(com * comb_raw, axis=1, keepdims=True))

    z_done(0)
    spread(0)
    yi0, xg0 = yin_send(0), xg_send(0)
    z_done(1)
    spread(1)
    arrive(xg0)
    xgf0 = xg_fwd(0)
    arrive(yi0)
    xi0 = xin_send(0)
    arrive(xgf0)
    yg0, own0 = yg_send(0)
    yi1, xg1 = yin_send(1), xg_send(1)
    arrive(xi0)
    xif0 = xin_fwd(0)
    arrive(xg1)
    xgf1 = xg_fwd(1)
    arrive(yi1)
    xi1 = xin_send(1)
    arrive(xgf1)
    yg1, own1 = yg_send(1)
    arrive(xif0)
    arrive(yg0)
    own0.wait()
    loads[4].wait()
    loads[5].wait()
    hidden(0)
    partial(0)
    rx0, rx0b = xr_send(0)
    arrive(xi1)
    xif1 = xin_fwd(1)
    out0 = grads(0)
    arrive(rx0)
    rxf0 = xr_fwd(0)
    arrive(xif1)
    arrive(yg1)
    own1.wait()
    hidden(1)
    partial(1)
    rx1, rx1b = xr_send(1)
    arrive(rx0b)
    arrive(rxf0)
    ry0 = yr_send(0)
    arrive(rx1)
    rxf1 = xr_fwd(1)
    out1 = grads(1)
    arrive(ry0)
    yr_sum(0)
    arrive(rx1b)
    arrive(rxf1)
    ry1 = yr_send(1)
    arrive(ry1)
    yr_sum(1)

    mb = one_hot(
        128, 128,
        lambda r: (((r >> 2) & 1) ^ rep) * 64 + ((r >> 1) & 1) * 32 + (r >> 3) * 2 + (r & 1),
    )
    back = nn(mb, bb[...].reshape(128, D)).reshape(16, 8, D)
    zbs[...] = jnp.concatenate([back[:, :, :HALF], back[:, :, HALF:]], axis=1).astype(BF)

    def zb_copy(k):
        to = (wide + k) % 16
        return rc(zbs.at[to], zbr.at[wide], zb_s.at[k], zb_r.at[k], dev_w(k))

    @pl.loop(1, 16)
    def _(k):
        zb_copy(k).start()

    zbr[wide] = zbs[wide]

    @pl.loop(1, 16)
    def _(k):
        zb_copy(k).wait_recv()

    recv = zbr[...].reshape(256, HALF)
    halves = []
    for h in range(2):
        q = one_hot(
            128, 256,
            lambda s: ((s >> 2) & 15) * 16 + h * 8 + (s >> 6) * 4 + (s & 3),
        )
        halves.append(nn(q, recv).astype(BF))
    slot_back = jnp.concatenate(halves, axis=1)
    disp_raw = nt(tok[...], slot_back)
    dis = dispatch[...]
    ldisp = dis * (disp_raw - jnp.sum(dis * disp_raw, axis=0, keepdims=True))
    lg = (lcomb[...] + ldisp).astype(BF)
    rt[...] = tn(tok[...], lg).reshape(16, 2, 40, 128)
    s1 = go(rc(rt.at[:, 1 - c], rr1, c_s, c_r, core_dev))
    gx[...] = (nt(lg, routing[...]) + nn(dis.astype(BF), slot_back)).astype(BF)
    outx = pltpu.make_async_copy(gx, gx_h.at[0], out_sem.at[4])
    outx.start()
    s1.wait_recv()
    hh[...] = (rt[:, c] + rr1[...]).reshape(4, 4, 40, 128)
    s2 = [
        go(rc(hh.at[:, (x + d) % 4], rr2.at[d - 1], s2_s.at[d], s2_r.at[d], dev_x(d)))
        for d in (1, 3, 2)
    ]
    arrive(s2)
    gg[...] = hh[:, x] + rr2[0] + rr2[1] + rr2[2]
    s3 = []
    for d in (1, 3, 2):
        yy = (y + d) % 4
        s3.append(
            go(rc(gg.at[(yy % 2) * 2 + yy // 2], rr3.at[d - 1], s3_s.at[d], s3_r.at[d], dev_y(d)))
        )
    arrive(s3)
    total = gg[(y % 2) * 2 + y // 2] + rr3[0] + rr3[1] + rr3[2]
    for i in range(8):
        ex[i, 0:5] = total[5 * i:5 * i + 5]

    def s4_copy(k):
        return rc(ex.at[k], rr4.at[z], s4_s.at[k], s4_r.at[z], (rep, nar * 2 + c, k))

    @pl.loop(0, 8)
    def _(k):
        own = jnp.logical_and(nar == z, k == nar)

        @pl.when(own)
        def _():
            rr4[z] = ex[k]

        @pl.when(jnp.logical_not(own))
        def _():
            s4_copy(k).start()

    @pl.loop(0, 8)
    def _(k):
        @pl.when(jnp.logical_not(jnp.logical_and(nar == z, k == z)))
        def _():
            rc(ex.at[0], rr4.at[k], s4_s.at[0], s4_r.at[k], core_dev).wait_recv()

    tot = rr4[0]
    for i in range(1, 8):
        tot = tot + rr4[i]
    gr_ref[...] = tot[0:5]

    @pl.loop(0, 8)
    def _(k):
        @pl.when(jnp.logical_not(jnp.logical_and(nar == z, k == nar)))
        def _():
            s4_copy(k).wait_send()

    @pl.loop(1, 16)
    def _(k):
        z_copy(0, k).wait_send()
        z_copy(1, k).wait_send()
        zb_copy(k).wait_send()

    for copy in pending:
        copy.wait_send()
    for copy in out0 + out1 + [outx]:
        copy.wait()


def local(tokens, routing, grad_out, slot_out, w_first, w_second):
    any_spec = pl.BlockSpec(memory_space=pl.ANY)
    v = pltpu.VMEM
    dma = pltpu.SemaphoreType.DMA
    return pl.pallas_call(
        kernel,
        out_shape=(
            jax.ShapeDtypeStruct((1, 256, D), BF),
            jax.ShapeDtypeStruct((5, 128), F32),
            jax.ShapeDtypeStruct((2, D, 512), BF),
            jax.ShapeDtypeStruct((2, 512, D), BF),
        ),
        in_specs=[any_spec] * 6,
        out_specs=(any_spec, pl.BlockSpec(memory_space=pltpu.VMEM), any_spec, any_spec),
        scratch_shapes=[
            v((256, D), BF), v((D, 128), BF), v((256, D), BF), v((128, D), BF),
            v((2, D, 512), BF), v((2, 512, D), BF),
            v((256, D), BF), v((2, D, 512), BF), v((2, 512, D), BF),
            v((256, 128), F32), v((256, 128), F32), v((256, 128), F32),
            v((2, 16, 16, HALF), BF), v((2, 16, 16, HALF), BF),
            v((2, 2, 32, D), BF), v((2, 4, 2, 32, D), BF), v((2, 2, 4, 4, 32, D), BF),
            v((2, 512, 512), BF), v((2, 512, 512), BF), v((2, 4, 4, 32, D), BF),
            v((2, 2, 2, 32, D), BF), v((2, 2, 4, 32, D), BF), v((2, 4, 32, D), BF),
            v((2, 3, 32, D), BF), v((2, 2, 32, D), BF), v((16, 16, HALF), BF), v((16, 16, HALF), BF),
            v((16, 2, 40, 128), F32), v((16, 40, 128), F32), v((4, 4, 40, 128), F32),
            v((3, 4, 40, 128), F32), v((4, 40, 128), F32), v((3, 40, 128), F32),
            v((8, 8, 128), F32), v((8, 8, 128), F32),
            dma((6,)), dma((5,)), dma((2,)),
            dma((2, 16)), dma((2, 16)), dma((2, 4)), dma((2, 4)), dma((2, 4)), dma((2, 4)),
            dma((2, 4)), dma((2, 4)), dma((2, 4)), dma((2, 4)),
            dma((2, 6)), dma((2, 6)), dma((2, 4)), dma((2, 4)), dma((16,)), dma((16,)),
            dma, dma, dma((4,)), dma((4,)), dma((4,)), dma((4,)), dma((8,)), dma((8,)),
        ],
        compiler_params=pltpu.CompilerParams(
            collective_id=0, has_side_effects=True, vmem_limit_bytes=56 * 2**20
        ),
    )(tokens, routing, grad_out, slot_out, w_first, w_second)


def solution(mesh):
    return jax.shard_map(
        local,
        mesh=mesh,
        in_specs=(
            P(("rep", "wide", "narrow"), None, None),
            P(),
            P(("rep", "wide", "narrow"), None, None),
            P(("rep", "wide", "narrow"), None, None),
            P(("rep", "wide"), None, "narrow"),
            P(("rep", "wide"), "narrow", None),
        ),
        out_specs=(
            P(("rep", "wide", "narrow"), None, None),
            P(("rep", "wide", "narrow"), None),
            P(("rep", "wide"), None, "narrow"),
            P(("rep", "wide"), "narrow", None),
        ),
        check_vma=False,
    )
```

time: 548 us -> 130 us (0.24)
  waiting for transfers between devices: 419 us -> 0 us
  Pallas kernels: 0 us -> 119 us
  blocking collectives: 41.5 us -> 0 us
  matrix products: 33.6 us -> 0 us
  local copies, waits for them, and re-layouts: 29.1 us -> 8.29 us
  between operations: 13.9 us -> 0.64 us
  starting transfers between devices: 9.69 us -> 0 us
    unnamed x5 -> x0, waiting for transfers between devices: 244 us -> none
    pallas_call x0 -> x1, Pallas kernels: none -> 119 us  [local(): pl.pallas_call(kernel, out_shape=(jax.ShapeDtypeStruct((1, 256, D), BF),...]
    all_gather x2 -> x0, waiting for transfers between devices: 89 us -> none  [the longest x1 47.4 us: local(): lax.all_gather(routed[1], 'narrow', axis=0, tiled=True)]
    reduce_scatter x1 -> x0, waiting for transfers between devices: 81.2 us -> none  [local(): lax.psum_scatter(jnp.einsum('ijsf,jdf->ijsd', hid_grad, w_first, preferre...]
    all_to_all x2 -> x0, blocking collectives: 41.5 us -> none  [the longest x1 23.9 us: local(): lax.all_to_all(slot_in, ('rep', 'wide'), split_axis=0, concat_axis=0, til...]
    dot_general x13 -> x0, matrix products: 33.6 us -> none  [the longest x1 5.19 us: local(): jnp.einsum('ijsd,jfd->ijsf', rows_grad, w_second, preferred_element_type=...]
    reshape x3 -> x0, local copies, waits for them, and re-layouts: 20.3 us -> none  [the longest x2 13.8 us: local(): rows_in = rows_in.reshape(narrow * groups, experts_here, slot_count, width)]
    all_to_all x1 -> x0, starting transfers between devices: 9.35 us -> none  [local(): lax.all_to_all(back_in, ('rep', 'wide'), split_axis=0, concat_axis=0, til...]
  transfers between devices with their start and end apart: 5 -> 0, of which waited for: 5 -> 0; matrix products, arithmetic and copies ran while one was open for 6% -> 0% of each run, Pallas kernels for 0% -> 0%
where the time goes in v1:
time: 130 us; the launch traced here: 128 us
  Pallas kernels  119 us (92%)
  local copies, waits for them, and re-layouts  8.29 us (6%)
    pallas_call x1, Pallas kernels, local(): pl.pallas_call(kernel, out_shape=(jax.ShapeDtypeStruct((1, 256, D), BF),...  119 us
    unnamed x6, local copies, waits for them, and re-layouts  8.29 us

profile of v1, /device:TPU:1, one launch (start us, length us, event | category | flops | bytes accessed | tf_op | source)
XLA Modules:
  0.0 128.0 jit_solution(11578692575659564949)
XLA Ops:
  0.6 119.1 %shard_map.93 = (bf16[1,256,1280]{2,1,0:T(8,128)(2,1)}, f32[5,128]{1,0:T(8,128)}, bf16[2,1280,512]{2,1,0:T(8,128)(2,1)}, bf16[2,512,1280]{2,1,0:T(8,128)(2,1)}) custom-call(bf16[1,256,1280]{2,1,0:T(8,128)(2,1)} %tok_h.1, bf16[1280,128]{1,0:T(8,128)(2,1)} %routing_h.1, bf16[1,256,1280]{2,1,0:T(8,128)(2,1)} %gout_h.1, bf16[1,128,1280]{2,1,0:T(8,128)(2,1)} %sout_h.1, ...), custom_call_target="tpu_custom_call" | custom-call | tf_op jit(solution)/shard_map/pallas_call | solution.py:436
  119.7 2.0 %copy.14 = bf16[1,256,1280]{2,1,0:T(8,128)(2,1)} copy(bf16[1,256,1280]{2,1,0:T(8,128)(2,1)} %get-tuple-element.8) | data formatting | bytes 1310720
  121.7 1.3 copy.15
  122.9 0.0 copy-start
  122.9 3.6 %copy.16 = bf16[2,1280,512]{2,1,0:T(8,128)(2,1)} copy(bf16[2,1280,512]{2,1,0:T(8,128)(2,1)} %get-tuple-element.10) | data formatting | bytes 5242880
  126.5 0.0 copy-done
  126.5 1.5 %copy.17 = bf16[2,512,1280]{2,1,0:T(8,128)(2,1)} copy(bf16[2,512,1280]{2,1,0:T(8,128)(2,1)S(1)} %copy-done) | data formatting | bytes 5242880
Async XLA Ops:
  122.9 3.6 %copy-start = (bf16[2,512,1280]{2,1,0:T(8,128)(2,1)S(1)}, bf16[2,512,1280]{2,1,0:T(8,128)(2,1)}, u32[]{:S(2)}) copy-start(bf16[2,512,1280]{2,1,0:T(8,128)(2,1)} %get-tuple-element.11) | copy-start | bytes 7864324

commit v2 on v1

v2 whole, which is shorter than its diff:
```python
import functools

import jax
import jax.numpy as jnp
from jax import lax
from jax.experimental import pallas as pl
from jax.experimental.pallas import tpu as pltpu
from jax.sharding import PartitionSpec as P

MESH = pl.DeviceIdType.MESH
BF = jnp.bfloat16
F32 = jnp.float32
root_half = 0.7071067811865476
density_scale = 0.3989422804014327
D = 1280
HALF = 640
LIMIT = 56
OUT = pltpu.VMEM


def nn(a, b):
    return lax.dot_general(a, b, (((1,), (0,)), ((), ())), preferred_element_type=F32)


def nt(a, b):
    return lax.dot_general(a, b, (((1,), (1,)), ((), ())), preferred_element_type=F32)


def tn(a, b):
    return lax.dot_general(a, b, (((0,), (0,)), ((), ())), preferred_element_type=F32)


def one_hot(rows, cols, pick):
    row = lax.broadcasted_iota(jnp.int32, (rows, cols), 0)
    col = lax.broadcasted_iota(jnp.int32, (rows, cols), 1)
    return (col == pick(row)).astype(F32).astype(BF)


def kernel(
    tok_h, routing_h, gout_h, sout_h, w1_h, w2_h,
    gx, gr_ref, g1, g2,
    tok, routing, gout, sout, w1, w2,
    dispatch, combine, lcomb,
    zs, zr, ai, xg, rows, act, hid, pb, xr1, xr2, xs, yr, yq, qs, bb, zbs, zbr,
    tokt, rt, rr, ex, rr4,
    ld_sem, loc_sem,
    zf_s, zf_r, yi_s, yi_r, xi_s, xi_r, xg_s, xg_r, yg_s, yg_r,
    rx_s, rx_r, ry_s, ry_r, zb_s, zb_r,
    pl_s, pl_r, s4_s, s4_r,
):
    rep = lax.axis_index("rep")
    wide = lax.axis_index("wide")
    nar = lax.axis_index("narrow")
    x = nar % 4
    y = (nar // 4) * 2 + rep
    z = wide // 2
    c = wide % 2

    def dev_x(d):
        return (rep, wide, (nar // 4) * 4 + (x + d) % 4)

    def dev_y(d):
        yy = (y + d) % 4
        return (yy % 2, wide, (yy // 2) * 4 + x)

    def dev_w(k):
        return (rep, (wide + k) % 16, nar)

    core_dev = (rep, z * 2 + 1 - c, nar)

    def rc(src, dst, ss, rs, dev):
        return pltpu.make_async_remote_copy(
            src_ref=src, dst_ref=dst, send_sem=ss, recv_sem=rs, device_id=dev, device_id_type=MESH
        )

    pending = []

    def go(copy):
        copy.start()
        pending.append(copy)
        return copy

    loads = [
        pltpu.make_async_copy(h, v, ld_sem.at[i])
        for i, (h, v) in enumerate(
            ((tok_h.at[0], tok), (routing_h, routing), (gout_h.at[0], gout), (sout_h.at[0], sout), (w1_h, w1), (w2_h, w2))
        )
    ]
    for copy in loads[:4]:
        copy.start()

    barrier = pltpu.get_barrier_semaphore()

    def greet(dev):
        pl.semaphore_signal(barrier, inc=1, device_id=dev, device_id_type=MESH)

    @pl.loop(1, 16)
    def _(k):
        greet(dev_w(k))

    @pl.loop(1, 32)
    def _(k):
        cc, xx, yy = (c + k) % 2, (x + k // 2) % 4, (y + k // 8) % 4
        greet((yy % 2, z * 2 + cc, (yy // 2) * 4 + xx))

    @pl.loop(1, 8)
    def _(k):
        greet(dev_w(2 * k))

    loads[0].wait()
    loads[1].wait()
    logits = nn(tok[...], routing[...])
    e0 = jnp.exp(logits - jnp.max(logits, axis=0, keepdims=True))
    dis = e0 / jnp.sum(e0, axis=0, keepdims=True)
    dispatch[...] = dis
    e1 = jnp.exp(logits - jnp.max(logits, axis=1, keepdims=True))
    com = e1 / jnp.sum(e1, axis=1, keepdims=True)
    combine[...] = com
    dis_bf = dis.astype(BF)
    com_bf = com.astype(BF)
    loads[2].wait()
    loads[4].start()
    loads[5].start()

    def z_copy(kind, j, k):
        to = (wide + k) % 16
        return rc(
            zs.at[kind, j, to], zr.at[kind, j, wide], zf_s.at[kind, j, k], zf_r.at[kind, j, k], dev_w(k)
        )

    def z_pack(kind, j):
        pt = one_hot(
            128, 128,
            lambda s: ((s >> 1) & 1) * 64 + (s >> 3) * 4 + j * 2 + (s & 1),
        )
        first = (lax.broadcasted_iota(jnp.int32, (128, HALF), 0) & 4) == 0
        probs, src = ((dis_bf, tok), (com_bf, gout))[kind]
        pick = nt(pt, probs).astype(BF)
        both = jnp.where(first, nn(pick, src[:, :HALF]), nn(pick, src[:, HALF:]))
        zs[kind, j] = both.reshape(16, 8, HALF).astype(BF)

    def z_send(kind, j):
        @pl.loop(1, 16)
        def _(k):
            z_copy(kind, j, k).start()

        zr[kind, j, wide] = zs[kind, j, wide]

    def z_done(kind, j):
        @pl.loop(1, 16)
        def _(k):
            z_copy(kind, j, k).wait_recv()

    def spread(kind, j):
        m = one_hot(
            128, 128,
            lambda r: ((r >> 1) & 15) * 8 + (r >> 6) * 4 + ((r >> 5) & 1) * 2 + (r & 1),
        )
        out = nn(m, zr[kind, j].astype(F32).reshape(128, HALF).astype(BF)).astype(BF)
        for h in range(2):
            cols = slice(h * HALF, (h + 1) * HALF)
            part = out[h * 64:h * 64 + 64].reshape(2, 32, HALF)
            if kind == 0:
                ai[j, :, :, cols] = part
            else:
                xg[j, x, :, :, cols] = part
        if kind == 0:
            rows[j, 0, x, y] = ai[j, rep]

    z_pack(1, 0)
    pl.semaphore_wait(barrier, 15 + 31 + 7)
    z_send(1, 0)
    z_pack(0, 0)
    z_send(0, 0)
    z_pack(1, 1)
    z_pack(0, 1)

    def yin_send(j):
        return {
            d: go(rc(ai.at[j, (y + d) % 2], rows.at[j, 0, x, y], yi_s.at[j, d], yi_r.at[j, d], dev_y(d)))
            for d in (1, 3, 2)
        }

    def xin_copy(j, e, source, way, sem):
        block = rows.at[j, 0, source, (y + 4 - e) % 4]
        return go(rc(block, block, xi_s.at[j, e, sem], xi_r.at[j, e, sem], dev_x(way)))

    def xin_send(j, e):
        return [xin_copy(j, e, x, 1, 0), xin_copy(j, e, x, 3, 1)]

    def xin_fwd(j, e, direct):
        if e < 2:
            direct[0].wait_recv()
            return xin_copy(j, e, (x + 3) % 4, 1, 2)
        direct[1].wait_recv()
        return xin_copy(j, e, (x + 1) % 4, 3, 2)

    def xg_send(j):
        return [
            go(rc(xg.at[j, x], xg.at[j, x], xg_s.at[j, d], xg_r.at[j, d], dev_x(d)))
            for d in (1, 3)
        ]

    def xg_fwd(j):
        a, b = (x + 3) % 4, (x + 1) % 4
        return [
            go(rc(xg.at[j, a, 0], xg.at[j, a, 0], xg_s.at[j, 0], xg_r.at[j, 0], dev_x(1))),
            go(rc(xg.at[j, b, 1], xg.at[j, b, 1], xg_s.at[j, 2], xg_r.at[j, 2], dev_x(3))),
        ]

    def yg_send(j, e):
        source = (x + e) % 4
        own = pltpu.make_async_copy(xg.at[j, source, rep], rows.at[j, 1, source, y], loc_sem.at[j, e])
        own.start()
        out = [
            go(rc(xg.at[j, source, (y + d) % 2], rows.at[j, 1, source, y],
                  yg_s.at[j, e, d], yg_r.at[j, e, d], dev_y(d)))
            for d in (1, 3, 2)
        ]
        return out, own

    def arrive(copies):
        for copy in copies:
            copy.wait_recv()

    def hidden(j):
        @pl.loop(0, 2)
        def _(i):
            cols = pl.ds(pl.multiple_of(i * 256, 256), 256)
            pre = nn(rows[j, 0].reshape(512, D), w1[j, :, cols])
            cdf = 0.5 * (1.0 + lax.erf(pre * root_half))
            act[j, :, cols] = (pre * cdf).astype(BF)
            slope = cdf + pre * (density_scale * jnp.exp(-0.5 * pre * pre))
            grad = nt(rows[j, 1].reshape(512, D), w2[j, cols, :])
            hid[j, :, cols] = (grad * slope).astype(BF)

    def partial(j, h):
        @pl.loop(0, 5)
        def _(i):
            at = pl.ds(pl.multiple_of(h * HALF + i * 128, 128), 128)
            cols = pl.ds(pl.multiple_of(i * 128, 128), 128)
            pb[j, h, :, :, :, cols] = nt(hid[j], w1[j, at, :]).astype(BF).reshape(4, 4, 32, 128)

    def grads(j):
        @pl.loop(0, 5)
        def _(i):
            cols = pl.ds(pl.multiple_of(i * 256, 256), 256)
            g1[j, cols, :] = tn(rows[j, 0, :, :, :, cols].reshape(512, 256), hid[j]).astype(BF)
            g2[j, :, cols] = tn(act[j], rows[j, 1, :, :, :, cols].reshape(512, 256)).astype(BF)

    far, up, dn = (x + 2) % 4, (x + 1) % 4, (x + 3) % 4
    lo, hi = pl.ds(0, 2), pl.ds(2, 2)

    def add(*refs):
        total = refs[0][...].astype(F32)
        for ref in refs[1:]:
            total = total + ref[...].astype(F32)
        return total.astype(BF)

    def px_send(j, h):
        v = pb.at[j, h]
        return [
            go(rc(v.at[far, lo], xr1.at[j, h, 0], rx_s.at[j, h, 0], rx_r.at[j, h, 0], dev_x(1))),
            go(rc(v.at[far, hi], xr1.at[j, h, 1], rx_s.at[j, h, 1], rx_r.at[j, h, 1], dev_x(3))),
            go(rc(v.at[up, hi], xr2.at[j, h, 0, hi], rx_s.at[j, h, 2], rx_r.at[j, h, 2], dev_x(1))),
            go(rc(v.at[dn, lo], xr2.at[j, h, 1, lo], rx_s.at[j, h, 3], rx_r.at[j, h, 3], dev_x(3))),
        ]

    def px_fwd(j, h, sent):
        v = pb.at[j, h]
        sent[0].wait_recv()
        v[up, lo] = add(v.at[up, lo], xr1.at[j, h, 0])
        a = go(rc(v.at[up, lo], xr2.at[j, h, 0, lo], rx_s.at[j, h, 4], rx_r.at[j, h, 4], dev_x(1)))
        sent[1].wait_recv()
        v[dn, hi] = add(v.at[dn, hi], xr1.at[j, h, 1])
        b = go(rc(v.at[dn, hi], xr2.at[j, h, 1, hi], rx_s.at[j, h, 5], rx_r.at[j, h, 5], dev_x(3)))
        return [a, b, sent[2], sent[3]]

    def py_send(j, h, sent):
        arrive(sent)
        xs[j, h] = add(pb.at[j, h, x], xr2.at[j, h, 0], xr2.at[j, h, 1])
        return [
            go(rc(xs.at[j, h, (y + d) % 4], yr.at[j, h, d - 1], ry_s.at[j, h, d], ry_r.at[j, h, d], dev_y(d)))
            for d in (1, 3, 2)
        ]

    def p_sum(j, h, sent):
        arrive(sent)
        bb[j, h, 0] = add(xs.at[j, h, y], yr.at[j, h, 1])
        bb[j, h, 1] = add(yr.at[j, h, 0], yr.at[j, h, 2])

    def qy_send(j, h):
        return [
            go(rc(pb.at[j, h, :, (y + d) % 4], yq.at[d - 1], ry_s.at[j, h, d], ry_r.at[j, h, d], dev_y(d)))
            for d in (1, 3, 2)
        ]

    def qx_send(j, h, sent):
        arrive(sent)
        qs[0] = add(pb.at[j, h, :, y], yq.at[1])
        qs[1] = add(yq.at[0], yq.at[2])
        return [
            go(rc(qs.at[0, far], xr1.at[j, h, 0, 0], rx_s.at[j, h, 0], rx_r.at[j, h, 0], dev_x(1))),
            go(rc(qs.at[1, far], xr1.at[j, h, 1, 0], rx_s.at[j, h, 1], rx_r.at[j, h, 1], dev_x(3))),
            go(rc(qs.at[1, up], xr2.at[j, h, 0, 1], rx_s.at[j, h, 2], rx_r.at[j, h, 2], dev_x(1))),
            go(rc(qs.at[0, dn], xr2.at[j, h, 1, 0], rx_s.at[j, h, 3], rx_r.at[j, h, 3], dev_x(3))),
        ]

    def qx_fwd(j, h, sent):
        sent[0].wait_recv()
        qs[0, up] = add(qs.at[0, up], xr1.at[j, h, 0, 0])
        a = go(rc(qs.at[0, up], xr2.at[j, h, 0, 0], rx_s.at[j, h, 4], rx_r.at[j, h, 4], dev_x(1)))
        sent[1].wait_recv()
        qs[1, dn] = add(qs.at[1, dn], xr1.at[j, h, 1, 0])
        b = go(rc(qs.at[1, dn], xr2.at[j, h, 1, 1], rx_s.at[j, h, 5], rx_r.at[j, h, 5], dev_x(3)))
        return [a, b, sent[2], sent[3]]

    def q_sum(j, h, sent):
        arrive(sent)
        for o in range(2):
            bb[j, h, o] = add(qs.at[o, x], xr2.at[j, h, 0, o], xr2.at[j, h, 1, o])

    def zb_copy(j, k):
        to = (wide + k) % 16
        return rc(zbs.at[j, to], zbr.at[j, wide], zb_s.at[j, k], zb_r.at[j, k], dev_w(k))

    def zb_send(j):
        mb = one_hot(
            128, 64,
            lambda r: (((r >> 1) & 1) ^ rep) * 32 + (r >> 3) * 2 + (r & 1),
        )
        first = (lax.broadcasted_iota(jnp.int32, (128, HALF), 0) & 4) == 0
        both = [nn(mb, bb[j, h].reshape(64, HALF)) for h in range(2)]
        zbs[j] = jnp.where(first, both[0], both[1]).reshape(16, 8, HALF).astype(BF)

        @pl.loop(1, 16)
        def _(k):
            zb_copy(j, k).start()

        zbr[j, wide] = zbs[j, wide]

    def zb_done(j):
        @pl.loop(1, 16)
        def _(k):
            zb_copy(j, k).wait_recv()

    def turn():
        @pl.loop(0, 5)
        def _(i):
            row = lax.broadcasted_iota(jnp.int32, (256, D), 0) + i * 256
            col = lax.broadcasted_iota(jnp.int32, (256, D), 1)
            piece = (row * 52429) >> 18
            k = row - piece * 5
            zz, nn_, cc, lo_ = piece & 7, (piece >> 3) & 7, (piece >> 6) & 1, piece >> 7
            want = (((lo_ * 8 + zz) * 2 + cc) * 8 + nn_) * 5 + k
            pick = (col == want).astype(F32).astype(BF)
            tokt[pl.ds(pl.multiple_of(i * 256, 256), 256), :] = nt(pick, tok[...]).astype(BF)

    loads[3].wait()
    comb_raw = nt(gout[...], sout[...])
    com = combine[...]
    lcomb[...] = com * (comb_raw - jnp.sum(com * comb_raw, axis=1, keepdims=True))

    def step1(j, t):
        arrive(t["xg"])
        t["xgf"] = xg_fwd(j)
        t["yg"] += [yg_send(j, 3), yg_send(j, 1)]

    def step2(j, t):
        for d in (1, 3, 2):
            t["yi"][d].wait_recv()
            t["xi"][d] = xin_send(j, d)

    def step3(j, t):
        arrive(t["xgf"])
        t["yg"].append(yg_send(j, 2))

    def step4(j, t):
        for e in (0, 1, 3, 2):
            t["xf"].append(xin_fwd(j, e, t["xi"][e]))

    def step5(j, t):
        for e in (0, 1):
            t["xi"][e][1].wait_recv()
        for e in (2, 3):
            t["xi"][e][0].wait_recv()
        arrive(t["xf"])
        for out, own in t["yg"]:
            arrive(out)
            own.wait()

    def start_g(j):
        return dict(xg=xg_send(j), yg=[yg_send(j, 0)], xf=[])

    def start_i(j, t):
        t["yi"] = yin_send(j)
        t["xi"] = {0: xin_send(j, 0)}

    z_done(1, 0)
    z_send(1, 1)
    spread(1, 0)
    t0 = start_g(0)
    z_done(0, 0)
    z_send(0, 1)
    spread(0, 0)
    start_i(0, t0)
    turn()
    step1(0, t0)
    step2(0, t0)
    step3(0, t0)
    z_done(1, 1)
    spread(1, 1)
    z_done(0, 1)
    spread(0, 1)
    step4(0, t0)
    t1 = start_g(1)
    start_i(1, t1)
    loads[4].wait()
    loads[5].wait()
    step5(0, t0)
    hidden(0)
    step1(1, t1)
    step2(1, t1)
    partial(0, 0)
    partial(0, 1)
    step3(1, t1)
    step4(1, t1)
    p00 = px_send(0, 0)
    p01 = px_send(0, 1)
    step5(1, t1)
    hidden(1)
    p00 = px_fwd(0, 0, p00)
    p01 = px_fwd(0, 1, p01)
    partial(1, 1)
    q1 = qy_send(1, 1)
    partial(1, 0)
    p10 = px_send(1, 0)
    p00 = py_send(0, 0, p00)
    p01 = py_send(0, 1, p01)
    grads(0)
    q1 = qx_send(1, 1, q1)
    p10 = px_fwd(1, 0, p10)
    p_sum(0, 0, p00)
    p_sum(0, 1, p01)
    zb_send(0)
    q1 = qx_fwd(1, 1, q1)
    p10 = py_send(1, 0, p10)
    q_sum(1, 1, q1)
    p_sum(1, 0, p10)
    zb_send(1)
    grads(1)
    zb_done(0)
    zb_done(1)

    recv = zbr[...].astype(F32).reshape(256, HALF).astype(BF)
    halves = []
    for h in range(2):
        q = one_hot(
            128, 256,
            lambda s: ((s >> 1) & 1) * 128 + ((s >> 2) & 15) * 8 + h * 4 + (s >> 6) * 2 + (s & 1),
        )
        halves.append(nn(q, recv).astype(BF))
    slot_back = jnp.concatenate(halves, axis=1)
    disp_raw = nt(tok[...], slot_back)
    dis = dispatch[...]
    ldisp = dis * (disp_raw - jnp.sum(dis * disp_raw, axis=0, keepdims=True))
    lg = (lcomb[...] + ldisp).astype(BF)
    rt[...] = nn(tokt[...], lg).reshape(32, 40, 128).astype(BF)

    def plane_copy(k):
        cc, xx, yy = (c + k) % 2, (x + k // 2) % 4, (y + k // 8) % 4
        block = (yy % 2) * 16 + cc * 8 + (yy // 2) * 4 + xx
        dev = (yy % 2, z * 2 + cc, (yy // 2) * 4 + xx)
        return rc(rt.at[block], rr.at[k], pl_s.at[k], pl_r.at[k], dev)

    @pl.loop(1, 32)
    def _(k):
        plane_copy(k).start()

    rr[0] = rt[rep * 16 + c * 8 + nar]
    gx[0] = (nt(lg, routing[...]) + nn(dis.astype(BF), slot_back)).astype(BF)

    @pl.loop(1, 32)
    def _(k):
        plane_copy(k).wait_recv()

    total = jnp.sum(rr[...].astype(F32), axis=0)
    for i in range(8):
        ex[i, 0:5] = total[5 * i:5 * i + 5]

    def s4_copy(k):
        return rc(ex.at[(z + k) % 8], rr4.at[k], s4_s.at[k], s4_r.at[k], dev_w(2 * k))

    @pl.loop(1, 8)
    def _(k):
        s4_copy(k).start()

    rr4[0] = ex[z]

    @pl.loop(1, 8)
    def _(k):
        s4_copy(k).wait_recv()

    tot = rr4[0]
    for i in range(1, 8):
        tot = tot + rr4[i]
    gr_ref[...] = tot[0:5]

    @pl.loop(1, 8)
    def _(k):
        s4_copy(k).wait_send()

    @pl.loop(1, 16)
    def _(k):
        for j in range(2):
            z_copy(0, j, k).wait_send()
            z_copy(1, j, k).wait_send()
            zb_copy(j, k).wait_send()

    @pl.loop(1, 32)
    def _(k):
        plane_copy(k).wait_send()

    for copy in pending:
        copy.wait_send()


def local(tokens, routing, grad_out, slot_out, w_first, w_second):
    in_hbm = pl.BlockSpec(memory_space=pltpu.HBM)
    in_vmem = pl.BlockSpec(memory_space=pltpu.VMEM)
    v = pltpu.VMEM
    dma = pltpu.SemaphoreType.DMA
    shapes = (
        ((1, 256, D), BF),
        ((5, 128), F32),
        ((2, D, 512), BF),
        ((2, 512, D), BF),
    )
    return pl.pallas_call(
        kernel,
        out_shape=tuple(OUT(*shape) for shape in shapes),
        in_specs=[in_hbm] * 6,
        out_specs=(in_vmem,) * 4,
        scratch_shapes=[
            v((256, D), BF), v((D, 128), BF), v((256, D), BF), v((128, D), BF),
            v((2, D, 512), BF), v((2, 512, D), BF),
            v((256, 128), F32), v((256, 128), F32), v((256, 128), F32),
            v((2, 2, 16, 8, HALF), BF), v((2, 2, 16, 8, HALF), BF),
            v((2, 2, 32, D), BF), v((2, 4, 2, 32, D), BF), v((2, 2, 4, 4, 32, D), BF),
            v((2, 512, 512), BF), v((2, 512, 512), BF), v((2, 2, 4, 4, 32, HALF), BF),
            v((2, 2, 2, 2, 32, HALF), BF), v((2, 2, 2, 4, 32, HALF), BF), v((2, 2, 4, 32, HALF), BF),
            v((2, 2, 3, 32, HALF), BF), v((3, 4, 32, HALF), BF), v((2, 4, 32, HALF), BF),
            v((2, 2, 2, 32, HALF), BF),
            v((2, 16, 8, HALF), BF), v((2, 16, 8, HALF), BF),
            v((D, 256), BF), v((32, 40, 128), BF), v((32, 40, 128), BF),
            v((8, 8, 128), F32), v((8, 8, 128), F32),
            dma((6,)), dma((2, 4)),
            dma((2, 2, 16)), dma((2, 2, 16)), dma((2, 4)), dma((2, 4)), dma((2, 4, 3)), dma((2, 4, 3)),
            dma((2, 4)), dma((2, 4)), dma((2, 4, 4)), dma((2, 4, 4)),
            dma((2, 2, 6)), dma((2, 2, 6)), dma((2, 2, 4)), dma((2, 2, 4)), dma((2, 16)), dma((2, 16)),
            dma((32,)), dma((32,)), dma((8,)), dma((8,)),
        ],
        compiler_params=pltpu.CompilerParams(
            collective_id=0, has_side_effects=True, vmem_limit_bytes=LIMIT * 2**20
        ),
    )(tokens, routing, grad_out, slot_out, w_first, w_second)

def solution(mesh):
    return jax.shard_map(
        local,
        mesh=mesh,
        in_specs=(
            P(("rep", "wide", "narrow"), None, None),
            P(),
            P(("rep", "wide", "narrow"), None, None),
            P(("rep", "wide", "narrow"), None, None),
            P(("rep", "wide"), None, "narrow"),
            P(("rep", "wide"), "narrow", None),
        ),
        out_specs=(
            P(("rep", "wide", "narrow"), None, None),
            P(("rep", "wide", "narrow"), None),
            P(("rep", "wide"), None, "narrow"),
            P(("rep", "wide"), "narrow", None),
        ),
        check_vma=False,
    )
```

time: 130 us -> 112 us (0.86); the launches traced: 128 us -> 112 us
  Pallas kernels: 119 us -> 107 us
  local copies, waits for them, and re-layouts: 8.29 us -> 4.41 us
    pallas_call x1, Pallas kernels: 119 us -> 107 us  [local(): pl.pallas_call(kernel, out_shape=tuple((OUT(*shape) for shape in shapes))...]
    unnamed x6 -> x4, local copies, waits for them, and re-layouts: 8.29 us -> 4.41 us
where the time goes in v2:
time: 112 us
  Pallas kernels  107 us (96%)
  local copies, waits for them, and re-layouts  4.41 us (4%)
    pallas_call x1, Pallas kernels, local(): pl.pallas_call(kernel, out_shape=tuple((OUT(*shape) for shape in shapes))...  107 us
    unnamed x4, local copies, waits for them, and re-layouts  4.41 us

profile of v2, /device:TPU:1, one launch (start us, length us, event | category | flops | bytes accessed | tf_op | source)
XLA Modules:
  0.0 111.7 jit_solution(8539414964791490864)
XLA Ops:
  0.6 106.7 %shard_map.93 = (bf16[1,256,1280]{2,1,0:T(8,128)(2,1)S(1)}, f32[5,128]{1,0:T(8,128)S(1)}, bf16[2,1280,512]{2,1,0:T(8,128)(2,1)S(1)}, bf16[2,512,1280]{2,1,0:T(8,128)(2,1)S(1)}) custom-call(bf16[1,256,1280]{2,1,0:T(8,128)(2,1)} %tok_h.1, bf16[1280,128]{1,0:T(8,128)(2,1)} %routing_h.1, bf16[1,256,1280]{2,1,0:T(8,128)(2,1)} %gout_h.1, ...), custom_call_target="tpu_custom_call" | custom-call | tf_op jit(solution)/shard_map/pallas_call | solution.py:539
  107.3 0.8 copy.14
  108.1 0.6 copy.15
  108.7 1.5 %copy.16 = bf16[2,1280,512]{2,1,0:T(8,128)(2,1)} copy(bf16[2,1280,512]{2,1,0:T(8,128)(2,1)S(1)} %get-tuple-element.6) | data formatting | bytes 5242880
  110.2 1.5 %copy.17 = bf16[2,512,1280]{2,1,0:T(8,128)(2,1)} copy(bf16[2,512,1280]{2,1,0:T(8,128)(2,1)S(1)} %get-tuple-element.7) | data formatting | bytes 5242880

commit v3 on v2

--- a/solution.py
+++ b/solution.py
@@ -103,10 +103,6 @@
         cc, xx, yy = (c + k) % 2, (x + k // 2) % 4, (y + k // 8) % 4
         greet((yy % 2, z * 2 + cc, (yy // 2) * 4 + xx))
 
-    @pl.loop(1, 8)
-    def _(k):
-        greet(dev_w(2 * k))
-
     loads[0].wait()
     loads[1].wait()
     logits = nn(tok[...], routing[...])
@@ -168,7 +164,7 @@
             rows[j, 0, x, y] = ai[j, rep]
 
     z_pack(1, 0)
-    pl.semaphore_wait(barrier, 15 + 31 + 7)
+    pl.semaphore_wait(barrier, 15 + 31)
     z_send(1, 0)
     z_pack(0, 0)
     z_send(0, 0)
@@ -429,15 +425,14 @@
     p01 = px_send(0, 1)
     step5(1, t1)
     hidden(1)
+    partial(1, 1)
+    q1 = qy_send(1, 1)
     p00 = px_fwd(0, 0, p00)
     p01 = px_fwd(0, 1, p01)
-    partial(1, 1)
-    q1 = qy_send(1, 1)
     partial(1, 0)
     p10 = px_send(1, 0)
     p00 = py_send(0, 0, p00)
     p01 = py_send(0, 1, p01)
-    grads(0)
     q1 = qx_send(1, 1, q1)
     p10 = px_fwd(1, 0, p10)
     p_sum(0, 0, p00)
@@ -448,6 +443,7 @@
     q_sum(1, 1, q1)
     p_sum(1, 0, p10)
     zb_send(1)
+    grads(0)
     grads(1)
     zb_done(0)
     zb_done(1)

time: 112 us -> 109 us (0.973)
  Pallas kernels: 107 us -> 104 us
    pallas_call x1, Pallas kernels: 107 us -> 104 us  [local(): pl.pallas_call(kernel, out_shape=tuple((OUT(*shape) for shape in shapes))...]
where the time goes in v3:
time: 109 us
  Pallas kernels  104 us (95%)
  local copies, waits for them, and re-layouts  4.41 us (4%)
    pallas_call x1, Pallas kernels, local(): pl.pallas_call(kernel, out_shape=tuple((OUT(*shape) for shape in shapes))...  104 us
    unnamed x4, local copies, waits for them, and re-layouts  4.41 us

profile of v3, /device:TPU:1, one launch (start us, length us, event | category | flops | bytes accessed | tf_op | source)
XLA Modules:
  0.0 109.4 jit_solution(2780023536111694973)
XLA Ops:
  0.6 104.3 %shard_map.93 = (bf16[1,256,1280]{2,1,0:T(8,128)(2,1)S(1)}, f32[5,128]{1,0:T(8,128)S(1)}, bf16[2,1280,512]{2,1,0:T(8,128)(2,1)S(1)}, bf16[2,512,1280]{2,1,0:T(8,128)(2,1)S(1)}) custom-call(bf16[1,256,1280]{2,1,0:T(8,128)(2,1)} %tok_h.1, bf16[1280,128]{1,0:T(8,128)(2,1)} %routing_h.1, bf16[1,256,1280]{2,1,0:T(8,128)(2,1)} %gout_h.1, ...), custom_call_target="tpu_custom_call" | custom-call | tf_op jit(solution)/shard_map/pallas_call | solution.py:535
  104.9 0.8 copy.14
  105.8 0.6 copy.15
  106.4 1.5 %copy.16 = bf16[2,1280,512]{2,1,0:T(8,128)(2,1)} copy(bf16[2,1280,512]{2,1,0:T(8,128)(2,1)S(1)} %get-tuple-element.6) | data formatting | bytes 5242880
  107.9 1.5 %copy.17 = bf16[2,512,1280]{2,1,0:T(8,128)(2,1)} copy(bf16[2,512,1280]{2,1,0:T(8,128)(2,1)S(1)} %get-tuple-element.7) | data formatting | bytes 5242880

commit v4 on v3

--- a/solution.py
+++ b/solution.py
@@ -433,8 +433,8 @@
     p10 = px_send(1, 0)
     p00 = py_send(0, 0, p00)
     p01 = py_send(0, 1, p01)
+    p10 = px_fwd(1, 0, p10)
     q1 = qx_send(1, 1, q1)
-    p10 = px_fwd(1, 0, p10)
     p_sum(0, 0, p00)
     p_sum(0, 1, p01)
     zb_send(0)

time: 109 us -> 108 us (level)
  no operation moved by 1% of the time
where the time goes in v4:
time: 108 us
  Pallas kernels  103 us (95%)
  local copies, waits for them, and re-layouts  4.41 us (4%)
    pallas_call x1, Pallas kernels, local(): pl.pallas_call(kernel, out_shape=tuple((OUT(*shape) for shape in shapes))...  103 us
    unnamed x4, local copies, waits for them, and re-layouts  4.41 us

profile of v4, /device:TPU:1, one launch (start us, length us, event | category | flops | bytes accessed | tf_op | source)
XLA Modules:
  0.0 108.4 jit_solution(407068740782459302)
XLA Ops:
  0.6 103.3 %shard_map.93 = (bf16[1,256,1280]{2,1,0:T(8,128)(2,1)S(1)}, f32[5,128]{1,0:T(8,128)S(1)}, bf16[2,1280,512]{2,1,0:T(8,128)(2,1)S(1)}, bf16[2,512,1280]{2,1,0:T(8,128)(2,1)S(1)}) custom-call(bf16[1,256,1280]{2,1,0:T(8,128)(2,1)} %tok_h.1, bf16[1280,128]{1,0:T(8,128)(2,1)} %routing_h.1, bf16[1,256,1280]{2,1,0:T(8,128)(2,1)} %gout_h.1, ...), custom_call_target="tpu_custom_call" | custom-call | tf_op jit(solution)/shard_map/pallas_call | solution.py:535
  104.0 0.8 copy.14
  104.8 0.6 copy.15
  105.4 1.5 %copy.16 = bf16[2,1280,512]{2,1,0:T(8,128)(2,1)} copy(bf16[2,1280,512]{2,1,0:T(8,128)(2,1)S(1)} %get-tuple-element.6) | data formatting | bytes 5242880
  106.9 1.5 %copy.17 = bf16[2,512,1280]{2,1,0:T(8,128)(2,1)} copy(bf16[2,512,1280]{2,1,0:T(8,128)(2,1)S(1)} %get-tuple-element.7) | data formatting | bytes 5242880
